TPU v7x, 32 devices: a whole 2x2x4 slice. The times are simulated.
32 devices in a mesh: tensor: 4 (over y, x), dp: 2 (over core), seq: 4 (over z).
Axes of the slice: x: 2, y: 2, z: 4, core: 2. Of those that a mesh axis runs over, the one named last changes fastest.
Arguments:
- tokens: bfloat16 [4, 2048, 1792], P('dp', 'seq'), may hold values from -6 to 6
- lengths: int32 [4], P('dp'), may hold values from 1024 to 2048, as said below
- attn_gain: float32 [1792], replicated, may hold values from 0.25 to 1.75
- w_query: bfloat16 [1792, 256], P(None, 'tensor'), may hold values from -0.125 to 0.125
- w_key: bfloat16 [1792, 256], P(None, 'tensor'), may hold values from -0.125 to 0.125
- w_value: bfloat16 [1792, 1792], P(None, 'tensor'), may hold values from -0.125 to 0.125
- w_output: bfloat16 [1792, 1792], P('tensor'), may hold values from -2 to 2
- mlp_gain: float32 [1792], replicated, may hold values from 0.25 to 1.75
- w_gate: bfloat16 [1792, 4864], P(None, 'tensor'), may hold values from -0.125 to 0.125
- w_up: bfloat16 [1792, 4864], P(None, 'tensor'), may hold values from -0.125 to 0.125
- w_down: bfloat16 [4864, 1792], P('tensor'), may hold values from -0.078125 to 0.078125
- cotangent: bfloat16 [4, 2048, 1792], P('dp', 'seq'), may hold values from -6 to 6
Outputs:
- block_out: bfloat16 [4, 2048, 1792], P('dp', 'seq')
- grad_tokens: float32 [4, 2048, 1792], P('dp', 'seq')
- grad_attn_gain: float32 [1792], P(('dp', 'seq'))
- grad_query: float32 [1792, 256], P(('dp', 'seq'), 'tensor')
- grad_key: float32 [1792, 256], P(('dp', 'seq'), 'tensor')
- grad_value: float32 [1792, 1792], P(('dp', 'seq'), 'tensor')
- grad_output: float32 [1792, 1792], P('tensor', ('dp', 'seq'))
- grad_mlp_gain: float32 [1792], P(('dp', 'seq'))
- grad_gate: float32 [1792, 4864], P(('dp', 'seq'), 'tensor')
- grad_up: float32 [1792, 4864], P(('dp', 'seq'), 'tensor')
- grad_down: float32 [4864, 1792], P('tensor', ('dp', 'seq'))
Inputs may be any that keep to these rules, and one draw needn't show every extreme that they name: `lengths`: among the 2 consecutive sequences that one index of dp holds, at least one has length 2048.
All inputs are finite; a program needn't handle non-finite values.
Results may differ from a plain program's by a relative error of at most 0.024.
Values may be sent and summed in bfloat16 or wider, within the bound.
A program may use at most 192 MiB of HBM per device.

v0:
```python
import math

import jax
import jax.numpy as jnp
import numpy as np
from jax import lax
from jax.sharding import PartitionSpec as P

F = 16


HIGHEST_PREC = lax.Precision.HIGHEST


def carried_in(x, axis, combine, identity, reverse):
    devices, index = (lax.axis_size(axis), lax.axis_index(axis))
    everything = jax.tree.map(
        lambda part, kind: lax.all_gather(part.astype(kind), axis),
        x,
        jax.tree.map(lambda a: jnp.bfloat16 if a.dtype == jnp.float32 else a.dtype, x),
    )
    start = jax.tree.map(
        lambda part, zero: jnp.broadcast_to(jnp.asarray(zero, part.dtype), part.shape), x, identity
    )

    def step(k, before):
        at = devices - 1 - k if reverse else k
        reached = at > index if reverse else at < index
        new = combine(
            before, jax.tree.map(lambda part, own: part[at].astype(own.dtype), everything, x)
        )
        return jax.tree.map(lambda a, b: jnp.where(reached, a, b), new, before)

    return lax.fori_loop(0, devices, step, start)


def rms_apply(row_data, gain_vec):
    return (
        row_data
        * lax.rsqrt(jnp.mean(row_data * row_data, axis=-1, keepdims=True) + 1e-06)
        * gain_vec
    )


def feature_map(values):
    upper_i, upper_j = np.triu_indices(F)
    pair_scale = np.where(upper_i == upper_j, 1.0 / math.sqrt(2.0 * F), 1.0 / math.sqrt(F)).astype(
        np.float32
    )
    constant = jnp.ones(values.shape[:-1] + (1,), values.dtype)
    pair_terms = values[..., upper_i] * values[..., upper_j] * pair_scale
    return jnp.concatenate([constant, values / F**0.25, pair_terms], axis=-1)


def attend_block(queries, key_rows, value_rows, kv_prefix, norm_prefix, raw_scores):
    scores = raw_scores / math.sqrt(F)
    block_len = queries.shape[1]
    causal = (
        lax.broadcasted_iota(jnp.int32, (block_len, block_len), 0)
        >= lax.broadcasted_iota(jnp.int32, (block_len, block_len), 1)
    ).astype(jnp.float32)
    weights = (1.0 + scores + 0.5 * scores * scores) * causal
    phi_query = feature_map(queries)
    numerator = jnp.einsum("bhtu,buhe->bthe", weights, value_rows, precision=HIGHEST_PREC)
    numerator = numerator + jnp.einsum(
        "bthm,bhme->bthe", phi_query, kv_prefix, precision=HIGHEST_PREC
    )
    denominator = jnp.swapaxes(jnp.sum(weights, axis=-1), 1, 2)
    denominator = denominator + jnp.einsum(
        "bthm,bhm->bth", phi_query, norm_prefix, precision=HIGHEST_PREC
    )
    return numerator / denominator[..., None]


def local_states(key_rows, value_rows):
    phi_key = feature_map(key_rows)
    kv_local = jnp.einsum("buhm,buhe->bhme", phi_key, value_rows, precision=HIGHEST_PREC)
    return (kv_local, jnp.sum(phi_key, axis=1))


def add_states(earlier, latter):
    return (earlier[0] + latter[0], earlier[1] + latter[1])


def product(left_side, right_side, form):
    return jnp.einsum(form, left_side, right_side, preferred_element_type=jnp.float32)


def shards(
    tokens,
    lengths,
    attn_gain,
    w_query,
    w_key,
    w_value,
    w_output,
    mlp_gain,
    w_gate,
    w_up,
    w_down,
    cotangent,
):
    seq_count, block_len, model_width = tokens.shape
    row_count = seq_count * block_len
    token_rows = tokens.reshape(row_count, model_width).astype(jnp.float32)
    heads_local = w_query.shape[1] // F
    head_value = w_value.shape[1] // heads_local
    positions = lax.axis_index("seq") * block_len + jnp.arange(block_len, dtype=jnp.int32)
    row_mask = (positions[None, :] < lengths[:, None]).astype(jnp.float32).reshape(row_count, 1)
    normed_attn, pull_attn_norm = jax.vjp(rms_apply, token_rows, attn_gain)
    normed_low = normed_attn.astype(jnp.bfloat16)
    queries = product(normed_low, w_query, "rd,dq->rq").astype(jnp.bfloat16)
    key_rows = product(normed_low, w_key, "rd,dq->rq").astype(jnp.bfloat16)
    value_rows = product(normed_low, w_value, "rd,dv->rv").astype(jnp.bfloat16)
    query_low_heads = queries.reshape(seq_count, block_len, heads_local, F)
    key_low_heads = key_rows.reshape(seq_count, block_len, heads_local, F)
    query_heads = query_low_heads.astype(jnp.float32)
    key_heads = key_low_heads.astype(jnp.float32)
    value_heads = value_rows.astype(jnp.float32).reshape(
        seq_count, block_len, heads_local, head_value
    )
    raw_scores = product(query_low_heads, key_low_heads, "bthf,buhf->bhtu")
    kv_local, pull_states = jax.vjp(local_states, key_heads, value_heads)
    identity = (jnp.zeros_like(kv_local[0]), jnp.zeros_like(kv_local[1]))
    kv_prefix, norm_prefix = carried_in(
        (kv_local[0], kv_local[1]), "seq", add_states, identity, False
    )
    attended, pull_attend = jax.vjp(
        attend_block, query_heads, key_heads, value_heads, kv_prefix, norm_prefix, raw_scores
    )
    attended_low = attended.reshape(row_count, heads_local * head_value).astype(jnp.bfloat16)
    attn_out = lax.psum(
        product(attended_low, w_output, "rv,ve->re").astype(jnp.bfloat16), "tensor"
    ).astype(jnp.float32)
    residual = token_rows + attn_out
    normed_mlp, pull_mlp_norm = jax.vjp(rms_apply, residual, mlp_gain)
    normed_mlp_low = normed_mlp.astype(jnp.bfloat16)
    gate_proj = product(normed_mlp_low, w_gate, "rd,df->rf")
    up_proj = product(normed_mlp_low, w_up, "rd,df->rf")
    sigmoid_gate = jax.nn.sigmoid(gate_proj)
    silu_gate = gate_proj * sigmoid_gate
    hidden = (silu_gate * up_proj).astype(jnp.bfloat16)
    mlp_out = lax.psum(product(hidden, w_down, "rf,fe->re").astype(jnp.bfloat16), "tensor").astype(
        jnp.float32
    )
    block_out = (row_mask * (residual + mlp_out)).reshape(tokens.shape).astype(jnp.bfloat16)
    grad_rows = cotangent.reshape(row_count, model_width).astype(jnp.float32) * row_mask
    grad_low = grad_rows.astype(jnp.bfloat16)
    grad_hidden = product(grad_low, w_down, "re,fe->rf")
    grad_down = product(hidden, grad_low, "rf,re->fe")
    grad_gate_low = (
        grad_hidden * up_proj * sigmoid_gate * (1.0 + gate_proj * (1.0 - sigmoid_gate))
    ).astype(jnp.bfloat16)
    grad_up_low = (grad_hidden * silu_gate).astype(jnp.bfloat16)
    grad_gate = product(normed_mlp_low, grad_gate_low, "rd,rf->df")
    grad_up = product(normed_mlp_low, grad_up_low, "rd,rf->df")
    mlp_term = product(grad_gate_low, w_gate, "rf,df->rd") + product(grad_up_low, w_up, "rf,df->rd")
    grad_normed_mlp = lax.psum(mlp_term.astype(jnp.bfloat16), "tensor").astype(jnp.float32)
    grad_mixed_norm, grad_mlp_gain = pull_mlp_norm(grad_normed_mlp)
    grad_mixed = grad_rows + grad_mixed_norm
    grad_attn_low = grad_mixed.astype(jnp.bfloat16)
    grad_output = product(attended_low, grad_attn_low, "rv,re->ve")
    grad_attended = product(grad_attn_low, w_output, "re,ve->rv").reshape(
        seq_count, block_len, heads_local, head_value
    )
    grad_q_heads, grad_k_out, grad_v_out, grad_kv_prefix, grad_norm_prefix, grad_raw = pull_attend(
        grad_attended
    )
    grad_q_heads = grad_q_heads + jnp.einsum(
        "bhtu,buhf->bthf", grad_raw, key_heads, precision=HIGHEST_PREC
    )
    grad_k_out = grad_k_out + jnp.einsum(
        "bhtu,bthf->buhf", grad_raw, query_heads, precision=HIGHEST_PREC
    )
    grad_kv_sum, grad_norm_sum = carried_in(
        (grad_kv_prefix, grad_norm_prefix), "seq", add_states, identity, True
    )
    grad_k_state, grad_v_state = pull_states((grad_kv_sum, grad_norm_sum))
    grad_q_low = grad_q_heads.reshape(row_count, heads_local * F).astype(jnp.bfloat16)
    grad_k_low = (
        (grad_k_out + grad_k_state).reshape(row_count, heads_local * F).astype(jnp.bfloat16)
    )
    grad_v_low = (
        (grad_v_out + grad_v_state)
        .reshape(row_count, heads_local * head_value)
        .astype(jnp.bfloat16)
    )
    grad_query = product(normed_low, grad_q_low, "rd,rq->dq")
    grad_key = product(normed_low, grad_k_low, "rd,rq->dq")
    grad_value = product(normed_low, grad_v_low, "rd,rv->dv")
    attn_term = (
        product(grad_q_low, w_query, "rq,dq->rd")
        + product(grad_k_low, w_key, "rq,dq->rd")
        + product(grad_v_low, w_value, "rv,dv->rd")
    )
    grad_normed_attn = lax.psum(attn_term.astype(jnp.bfloat16), "tensor").astype(jnp.float32)
    grad_rows_norm, grad_attn_gain = pull_attn_norm(grad_normed_attn)
    grad_tokens = (grad_mixed + grad_rows_norm).reshape(tokens.shape)
    reduced = (
        lax.psum_scatter(
            grad_attn_gain.astype(jnp.bfloat16), ("dp", "seq"), scatter_dimension=0, tiled=True
        ).astype(jnp.float32),
        lax.psum_scatter(
            grad_query.astype(jnp.bfloat16), ("dp", "seq"), scatter_dimension=0, tiled=True
        ).astype(jnp.float32),
        lax.psum_scatter(
            grad_key.astype(jnp.bfloat16), ("dp", "seq"), scatter_dimension=0, tiled=True
        ).astype(jnp.float32),
        lax.psum_scatter(
            grad_value.astype(jnp.bfloat16), ("dp", "seq"), scatter_dimension=0, tiled=True
        ).astype(jnp.float32),
        lax.psum_scatter(
            grad_output.astype(jnp.bfloat16), ("dp", "seq"), scatter_dimension=1, tiled=True
        ).astype(jnp.float32),
        lax.psum_scatter(
            grad_mlp_gain.astype(jnp.bfloat16), ("dp", "seq"), scatter_dimension=0, tiled=True
        ).astype(jnp.float32),
        lax.psum_scatter(
            grad_gate.astype(jnp.bfloat16), ("dp", "seq"), scatter_dimension=0, tiled=True
        ).astype(jnp.float32),
        lax.psum_scatter(
            grad_up.astype(jnp.bfloat16), ("dp", "seq"), scatter_dimension=0, tiled=True
        ).astype(jnp.float32),
        lax.psum_scatter(
            grad_down.astype(jnp.bfloat16), ("dp", "seq"), scatter_dimension=1, tiled=True
        ).astype(jnp.float32),
    )
    return (
        block_out,
        grad_tokens,
        reduced[0],
        reduced[1],
        reduced[2],
        reduced[3],
        reduced[4],
        reduced[5],
        reduced[6],
        reduced[7],
        reduced[8],
    )


def solution(mesh):
    in_specs = (
        P("dp", "seq", None),
        P("dp"),
        P(),
        P(None, "tensor"),
        P(None, "tensor"),
        P(None, "tensor"),
        P("tensor", None),
        P(),
        P(None, "tensor"),
        P(None, "tensor"),
        P("tensor", None),
        P("dp", "seq", None),
    )
    out_specs = (
        P("dp", "seq", None),
        P("dp", "seq", None),
        P(("dp", "seq")),
        P(("dp", "seq"), "tensor"),
        P(("dp", "seq"), "tensor"),
        P(("dp", "seq"), "tensor"),
        P("tensor", ("dp", "seq")),
        P(("dp", "seq")),
        P(("dp", "seq"), "tensor"),
        P(("dp", "seq"), "tensor"),
        P("tensor", ("dp", "seq")),
    )
    return jax.shard_map(shards, mesh=mesh, in_specs=in_specs, out_specs=out_specs, check_vma=False)
```

profile of v0, /device:TPU:0, one launch (start us, length us, event | category | flops | bytes accessed | tf_op | source)
XLA Modules:
  0.0 1156.1 jit_solution(11739210626293032491)
XLA Ops:
  41.1 10.2 fusion.20
  57.3 14.8 %all-gather.1 = bf16[8,4,153]{2,1,0:T(4,128)(2,1)S(1)} all-gather(bf16[2,4,153]{2,1,0:T(4,128)(2,1)S(1)} %fusion.42), channel_id=3, replica_groups=mesh['tensor'=4,'dp'=2,'seq'=4] {'seq'}, dimensions={0}, use_global_device_ids=true | all-gather | bytes 12240 | tf_op jit(solution)/shard_map/all_gather | solution.py:18
  78.2 15.2 %fusion.45 = f32[2,4,112,512]{3,2,1,0:T(8,128)} fusion(f32[2,4,512,512]{2,3,1,0:T(8,128)S(1)} %get-tuple-element.386, f32[512,512]{0,1:T(8,128)S(1)} %fusion.59, bf16[2,512,4,112]{1,0,3,2:T(2,128)(2,1)S(1)} %copy-done.20), kind=kOutput, calls=%fused_computation.107 | convolution fusion | flops 2831155200 | bytes 12189696 | tf_op jit(solution)/shard_map/jvp(bhtu,buhe->bthe)/dot_general | solution.py:64
  119.2 92.0 %all-reduce.8.cloned.1.call-done = bf16[1024,1792]{1,0:T(8,128)(2,1)} async-done(((bf16[1024,1792]{1,0:T(8,128)(2,1)}), bf16[1024,1792]{1,0:T(8,128)(2,1)}) %all-reduce.8.cloned.1.call-update) | async-done | bytes 3670032 | tf_op jit(solution)/shard_map/psum | solution.py:132
  217.9 10.0 fusion.88
  234.4 11.8 %multiply_convert_fusion.2 = (bf16[1024,1216]{0,1:T(8,128)(2,1)S(1)}, bf16[1024,1216]{0,1:T(8,128)(2,1)S(1)}, bf16[1024,1216]{0,1:T(8,128)(2,1)}) fusion(f32[1024,1216]{0,1:T(8,128)} %fusion.87, f32[1024,1216]{0,1:T(8,128)} %fusion.88, bf16[1024,1792]{1,0:T(8,128)(2,1)S(1)} %copy-done.17, bf16[1216,1792]{1,0:T(8,128)(2,1)} %param.36), kind=kOutput, calls=%fused_computation.56 | convolution fusion | flops 4481417216 | bytes 25460736 | tf_op jit(solution)/shard_map/re,fe->rf/dot_general | solution.py:86
  263.8 91.2 %all-reduce.10.cloned.1.call-done = bf16[1024,1792]{1,0:T(8,128)(2,1)} async-done(((bf16[1024,1792]{1,0:T(8,128)(2,1)}), bf16[1024,1792]{1,0:T(8,128)(2,1)}) %all-reduce.10.cloned.1.call-update) | async-done | bytes 3670032 | tf_op jit(solution)/shard_map/psum | solution.py:158
  393.9 13.4 %all-gather.3 = bf16[8,4,153]{2,1,0:T(4,128)(2,1)S(1)} all-gather(bf16[2,4,153]{2,1,0:T(4,128)(2,1)S(1)} %bitcast.266), channel_id=5, replica_groups=mesh['tensor'=4,'dp'=2,'seq'=4] {'seq'}, dimensions={0}, use_global_device_ids=true | all-gather | bytes 12240 | tf_op jit(solution)/shard_map/all_gather | solution.py:18
  407.3 10.4 fusion.5
  427.3 11.3 fusion.24
  446.0 15.9 %scatter_fusion.2 = f32[2,512,4,16]{1,2,3,0:T(4,128)S(1)} fusion(f32[2,512,4,16]{1,2,3,0:T(4,128)S(1)} %copy.132, s32[136]{0:T(256)S(1)} %copy-done.45, f32[136,2,512,4]{2,3,1,0:T(4,128)} %copy.133), kind=kCustom, calls=%fused_computation.6 | custom fusion | flops 557056 | bytes 6685216 | tf_op jit(solution)/shard_map/transpose(jvp())/scatter-add | solution.py:51
  461.9 15.4 %scatter_fusion.3 = f32[2,512,4,16]{1,2,3,0:T(4,128)S(1)} fusion(f32[2,512,4,16]{1,2,3,0:T(4,128)S(1)} %broadcast.146.clone.1, s32[136]{0:T(256)S(1)} %copy-done.44, f32[136,2,512,4]{2,3,1,0:T(4,128)} %copy.134), kind=kCustom, calls=%fused_computation.7 | custom fusion | flops 557056 | bytes 6685216 | tf_op jit(solution)/shard_map/transpose(jvp())/scatter-add | solution.py:51
  495.6 15.3 %scatter_fusion.1 = f32[2,512,4,16]{1,2,3,0:T(4,128)S(1)} fusion(f32[2,512,4,16]{1,2,3,0:T(4,128)S(1)} %broadcast.146.clone, s32[136]{0:T(256)S(1)} %copy-done.44, f32[136,2,512,4]{2,3,1,0:T(4,128)} %copy.119), kind=kCustom, calls=%fused_computation.5 | custom fusion | flops 557056 | bytes 6685216 | tf_op jit(solution)/shard_map/transpose(jvp())/scatter-add | solution.py:51
  510.9 15.9 %scatter_fusion = f32[2,512,4,16]{1,2,3,0:T(4,128)S(1)} fusion(f32[2,512,4,16]{1,2,3,0:T(4,128)S(1)} %copy.117, s32[136]{0:T(256)S(1)} %copy-done.45, f32[136,2,512,4]{2,3,1,0:T(4,128)} %copy.118), kind=kCustom, calls=%fused_computation.4 | custom fusion | flops 557056 | bytes 6685216 | tf_op jit(solution)/shard_map/transpose(jvp())/scatter-add | solution.py:51
  549.4 13.4 %fusion.46 = bf16[2,512,4,112]{1,3,2,0:T(8,128)(2,1)S(1)} fusion(f32[2,4,112,512]{3,2,1,0:T(8,128)S(1)} %fusion.41, f32[2,4,512,512]{2,3,1,0:T(8,128)} %copy-done.50, f32[512,512]{0,1:T(8,128)S(1)} %copy-done.29, f32[2,512,4,112]{1,0,3,2:T(2,128)} %reshape.194, f32[2,512,4]{1,2,0:T(4,128)S(1)} %get-tuple-element.367), kind=kOutput, calls=%fused_computation.108 | convolution fusion | flops 2832531456 | bytes 14041088 | tf_op jit(solution)/shard_map/transpose(jvp(bhtu,buhe->bthe))/dot_general | solution.py:64
  578.5 10.0 convolution_convert_fusion.1
  588.6 10.1 convolution_convert_fusion.2
  622.4 35.2 %reduce-scatter.14.cloned.1.call-done = bf16[224,448]{1,0:T(8,128)(2,1)} async-done(((bf16[1792,448]{1,0:T(8,128)(2,1)}), bf16[224,448]{1,0:T(8,128)(2,1)}) %reduce-scatter.14.cloned.1.call-update) | async-done | bytes 200720 | tf_op jit(solution)/shard_map/reduce_scatter | solution.py:209
  659.3 96.0 %reduce-scatter.20.cloned.1.call-done = bf16[1216,224]{0,1:T(8,128)(2,1)} async-done(((bf16[1216,1792]{0,1:T(8,128)(2,1)}), bf16[1216,224]{0,1:T(8,128)(2,1)}) %reduce-scatter.20.cloned.1.call-update) | async-done | bytes 544784 | tf_op jit(solution)/shard_map/reduce_scatter | solution.py:224
  757.4 96.5 %reduce-scatter.18.cloned.1.call-done = bf16[224,1216]{1,0:T(8,128)(2,1)} async-done(((bf16[1792,1216]{1,0:T(8,128)(2,1)}), bf16[224,1216]{1,0:T(8,128)(2,1)}) %reduce-scatter.18.cloned.1.call-update) | async-done | bytes 544784 | tf_op jit(solution)/shard_map/reduce_scatter | solution.py:221
  856.0 96.5 %reduce-scatter.16.cloned.1.call-done = bf16[224,1216]{1,0:T(8,128)(2,1)} async-done(((bf16[1792,1216]{1,0:T(8,128)(2,1)}), bf16[224,1216]{1,0:T(8,128)(2,1)}) %reduce-scatter.16.cloned.1.call-update) | async-done | bytes 544784 | tf_op jit(solution)/shard_map/reduce_scatter | solution.py:218
  954.7 158.2 %all-reduce.12.cloned.1.call-done = (bf16[1024,1792]{1,0:T(8,128)(2,1)}, bf16[1024,1792]{1,0:T(8,128)(2,1)}) async-done(((bf16[1024,1792]{1,0:T(8,128)(2,1)}, bf16[1024,1792]{1,0:T(8,128)(2,1)}), (bf16[1024,1792]{1,0:T(8,128)(2,1)}, bf16[1024,1792]{1,0:T(8,128)(2,1)})) %all-reduce.12.cloned.1.call-update) | async-done | bytes 7340048 | tf_op jit(solution)/shard_map/psum | solution.py:143
  1118.2 17.2 %all-reduce.2 = (bf16[1792]{0:T(1024)(128)(2,1)S(1)}, bf16[1792]{0:T(1024)(128)(2,1)S(1)}) all-reduce(bf16[1792]{0:T(1024)(128)(2,1)S(1)} %get-tuple-element.336, bf16[1792]{0:T(1024)(128)(2,1)S(1)} %get-tuple-element.334), channel_id=6, replica_groups=mesh['tensor'=4,'dp'=2,'seq'=4] {'dp','seq'}, use_global_device_ids=true, to_apply=%region_20.21.clone | all-reduce | flops 3584 | bytes 14336
  1136.1 12.8 %fusion.11 = (f32[1024,1792]{1,0:T(8,128)}, bf16[1024,1792]{1,0:T(8,128)(2,1)}) fusion(f32[1024,1792]{1,0:T(8,128)} %copy-done.12, bf16[1024,1792]{1,0:T(8,128)(2,1)} %get-tuple-element.365, bf16[2,512,1792]{2,1,0:T(8,128)(2,1)} %param.26, f32[1024]{0:T(1024)S(1)} %multiply_multiply_fusion, f32[1792]{0:T(1024)S(1)} %copy-done.38, f32[1024]{0:T(1024)S(1)} %copy-done.41, ...), kind=kLoop, calls=%fused_computation.38 | loop fusion | flops 25690112 | bytes 33049600 | tf_op jit(solution)/shard_map/add | solution.py:198
  (279 shorter events, 261.4 us)
Async XLA Ops:
  7.2 102.8 %copy-start = (bf16[448,1792]{1,0:T(8,128)(2,1)S(1)}, bf16[448,1792]{1,0:T(8,128)(2,1)}, u32[]{:S(2)}) copy-start(bf16[448,1792]{1,0:T(8,128)(2,1)} %param.32) | copy-start | bytes 4816900
  7.2 86.2 %all-gather.7.cloned.1.call-start = ((), (), s32[]{:S(2)}) async-start(), calls=%async_computation.13 | async-start | bytes 1566720 | tf_op jit(solution)/shard_map/all_gather | solution.py:18
  15.0 40.2 %copy-start.23 = (f32[2,512,4,16]{1,3,2,0:T(8,128)}, f32[2,512,4,16]{1,3,2,0:T(8,128)S(1)}, u32[]{:S(2)}) copy-start(f32[2,512,4,16]{1,3,2,0:T(8,128)S(1)} %broadcast_multiply_fusion.1) | copy-start | bytes 786436
  55.1 156.1 %all-reduce.8.cloned.1.call-start = ((), (), s32[]{:S(2)}) async-start(), calls=%async_computation.7 | async-start | bytes 7340032 | tf_op jit(solution)/shard_map/psum | solution.py:132
  72.3 29.7 %copy-start.36 = (f32[2,512,4,16]{1,3,2,0:T(8,128)}, f32[2,512,4,16]{1,3,2,0:T(8,128)S(1)}, u32[]{:S(2)}) copy-start(f32[2,512,4,16]{1,3,2,0:T(8,128)S(1)} %broadcast_multiply_fusion) | copy-start | bytes 786436
  113.9 241.1 %all-reduce.10.cloned.1.call-start = ((), (), s32[]{:S(2)}) async-start(), calls=%async_computation.8 | async-start | bytes 7340032 | tf_op jit(solution)/shard_map/psum | solution.py:158
  119.2 96.6 %copy-start.39 = (f32[1792]{0:T(1024)S(1)}, f32[1792]{0:T(1024)}, u32[]{:S(2)}) copy-start(f32[1792]{0:T(1024)} %param.33) | copy-start | bytes 21508
  216.5 11.4 slice-start
  228.0 23.5 %slice-start.2 = ((s8[4358144]{0:T(1024)(128)(4,1)}), s8[4194304]{0:T(1024)(128)(4,1)S(1)}, s32[]{:S(2)}) async-start(s8[4358144]{0:T(1024)(128)(4,1)} %bitcast.269), calls=%async_computation.21 | async-start | bytes 8388608
  234.3 17.2 %slice-start.3 = ((s8[4358144]{0:T(1024)(128)(4,1)}), s8[163840]{0:T(1024)(128)(4,1)S(1)}, s32[]{:S(2)}) async-start(s8[4358144]{0:T(1024)(128)(4,1)} %bitcast.269), calls=%async_computation.22 | async-start | bytes 327680
  258.8 161.1 %all-gather.9.cloned.1.call-start = ((), (), s32[]{:S(2)}) async-start(), calls=%async_computation.14 | async-start | bytes 1566720 | tf_op jit(solution)/shard_map/all_gather | solution.py:18
  387.8 229.6 %reduce-scatter.24.cloned.1.call-start = ((), (), s32[]{:S(2)}) async-start(), calls=%async_computation.16 | async-start | bytes 516096
  387.8 19.5 %copy-start.16 = (f32[2,512,4,112]{1,0,3,2:T(2,128)S(1)}, f32[2,512,4,112]{1,0,3,2:T(2,128)}, u32[]{:S(2)}) copy-start(f32[2,512,4,112]{1,0,3,2:T(2,128)} %reshape.194) | copy-start | bytes 5505028
  387.8 19.5 %copy-start.21 = (bf16[2,512,4,112]{1,0,3,2:T(2,128)(2,1)S(1)}, bf16[2,512,4,112]{1,0,3,2:T(2,128)(2,1)}, u32[]{:S(2)}) copy-start(bf16[2,512,4,112]{1,0,3,2:T(2,128)(2,1)} %copy-done.19) | copy-start | bytes 2752516
  387.8 19.5 %copy-start.28 = (f32[512,512]{0,1:T(8,128)S(1)}, f32[512,512]{0,1:T(8,128)}, u32[]{:S(2)}) copy-start(f32[512,512]{0,1:T(8,128)} %copy-done.27) | copy-start | bytes 3145732
  486.7 132.3 %reduce-scatter.22.cloned.1.call-start = ((), (), s32[]{:S(2)}) async-start(), calls=%async_computation.15 | async-start | bytes 516096
  535.1 85.4 %reduce-scatter.26.cloned.1.call-start = ((), (), s32[]{:S(2)}) async-start(), calls=%async_computation.17 | async-start | bytes 2064384
  545.0 112.5 %reduce-scatter.14.cloned.1.call-start = ((), (), s32[]{:S(2)}) async-start(), calls=%async_computation.9 | async-start | bytes 2064384 | tf_op jit(solution)/shard_map/reduce_scatter | solution.py:209
  568.5 186.8 %reduce-scatter.20.cloned.1.call-start = ((), (), s32[]{:S(2)}) async-start(), calls=%async_computation.12 | async-start | bytes 5160960 | tf_op jit(solution)/shard_map/reduce_scatter | solution.py:224
  578.4 275.4 %reduce-scatter.18.cloned.1.call-start = ((), (), s32[]{:S(2)}) async-start(), calls=%async_computation.11 | async-start | bytes 5160960 | tf_op jit(solution)/shard_map/reduce_scatter | solution.py:221
  588.5 364.0 %reduce-scatter.16.cloned.1.call-start = ((), (), s32[]{:S(2)}) async-start(), calls=%async_computation.10 | async-start | bytes 5160960 | tf_op jit(solution)/shard_map/reduce_scatter | solution.py:218
  598.7 514.2 %all-reduce.12.cloned.1.call-start = ((), (), s32[]{:S(2)}) async-start(), calls=%async_computation.18 | async-start | bytes 14680064 | tf_op jit(solution)/shard_map/psum | solution.py:143
  617.3 495.6 %copy-start.41 = (f32[1024]{0:T(1024)S(1)}, f32[1024]{0:T(1024)}, u32[]{:S(2)}) copy-start(f32[1024]{0:T(1024)} %copy-done.40) | copy-start | bytes 12292
  1136.1 12.8 %copy-start.1 = (bf16[448,1792]{1,0:T(8,128)(2,1)S(1)}, bf16[448,1792]{1,0:T(8,128)(2,1)}, u32[]{:S(2)}) copy-start(bf16[448,1792]{1,0:T(8,128)(2,1)} %param.32) | copy-start | bytes 4816900
  (45 other events, 188.3 us)
Sparse Core Ops, SparseCore 0:
  55.2 34.5 all-gather.6
  114.0 97.1 all-reduce.7
  259.0 95.9 all-reduce.9
  387.9 31.9 all-gather.8
  486.8 31.3 reduce-scatter.23
  535.2 31.3 reduce-scatter.21
  568.9 42.9 reduce-scatter.25
  614.2 43.2 reduce-scatter.13
  659.9 95.3 reduce-scatter.19
  757.6 96.2 reduce-scatter.17
  856.2 96.2 reduce-scatter.15
  956.9 155.9 all-reduce.11
where the time goes:
time: 1170 us; the launch traced here: 1160 us
  waiting for transfers between devices  668 us (57%)
  matrix products  198 us (17%)
  other arithmetic  149 us (13%)
  local copies, waits for them, and re-layouts  77.5 us (7%)
  blocking collectives  45.5 us (4%)
  between operations  16.3 us (1%)
    psum x1, waiting for transfers between devices, shards(): lax.psum(product(hidden, w_down, 'rf,fe->re').astype(jnp.bfloat16), 'tens...  158 us
    dot_general x22, matrix products, product(): jnp.einsum(form, left_side, right_side, preferred_element_type=jnp.float32)  118 us
    reduce_scatter x1, waiting for transfers between devices, shards(): lax.psum_scatter(grad_gate.astype(jnp.bfloat16), ('dp', 'seq'), scatter_d...  96.5 us
    reduce_scatter x1, waiting for transfers between devices, shards(): lax.psum_scatter(grad_up.astype(jnp.bfloat16), ('dp', 'seq'), scatter_dim...  96.5 us
    reduce_scatter x1, waiting for transfers between devices, shards(): lax.psum_scatter(grad_down.astype(jnp.bfloat16), ('dp', 'seq'), scatter_d...  96 us
    psum x1, waiting for transfers between devices, shards(): lax.psum(product(attended_low, w_output, 'rv,ve->re').astype(jnp.bfloat16...  92 us
    psum x1, waiting for transfers between devices, shards(): lax.psum(mlp_term.astype(jnp.bfloat16), 'tensor').astype(jnp.float32)  91.2 us
    scatter-add x4, other arithmetic, feature_map(): pair_terms = values[..., upper_i] * values[..., upper_j] * pair_scale  62.5 us
  transfers between devices with their start and end apart: 12, of which 8 were waited for; matrix products, arithmetic and copies ran while one was open for 16% of the time, Pallas kernels for 0%

commit v1 on v0

v1 whole, which is shorter than its diff:
```python
import functools
import math

import jax
import jax.numpy as jnp
import numpy as np
from jax import lax
from jax.experimental import pallas as pl
from jax.experimental.pallas import tpu as pltpu
from jax.sharding import PartitionSpec as P

F = 16
FEATS = 160
LANES = 128
WIDE = 256
VMEM_LIMIT = 62 << 20
MESH = pl.DeviceIdType.MESH
BF16 = jnp.bfloat16
F32 = jnp.float32
VMEM_SPEC = pl.BlockSpec(memory_space=pltpu.VMEM)
ANY_SPEC = pl.BlockSpec(memory_space=pl.ANY)
NN = (((1,), (0,)), ((), ()))
NT = (((1,), (1,)), ((), ()))
TN = (((0,), (0,)), ((), ()))


def dot(a, b, dims=NN):
    return lax.dot_general(a, b, dims, preferred_element_type=F32)


def feature_tables(heads):
    upper_i, upper_j = np.triu_indices(F)
    pairs = len(upper_i)
    first = np.zeros((2 * heads * F, heads * WIDE), np.float32)
    second = np.zeros_like(first)
    rows = np.zeros((8, WIDE), np.float32)
    cols = np.arange(pairs)
    for h in range(heads):
        first[h * F + upper_i, h * WIDE + cols] = 1.0
        second[h * F + upper_j, h * WIDE + cols] = 1.0
        first[h * F + np.arange(F), h * WIDE + pairs + np.arange(F)] = 1.0
    rows[0, pairs + F] = 1.0
    rows[1, pairs : pairs + F + 1] = 1.0
    rows[2, :pairs] = np.where(upper_i == upper_j, 1.0 / (2 * F), 1.0 / F)
    rows[2, pairs : pairs + F] = 1.0 / math.sqrt(F)
    rows[2, pairs + F] = 1.0
    return tuple(jnp.asarray(a, BF16) for a in (first, second)) + (jnp.asarray(rows),)


def spread_table(heads, width):
    table = np.zeros((heads * width, heads * LANES), np.float32)
    for h in range(heads):
        table[h * width + np.arange(width), h * LANES + np.arange(width)] = 1.0
    return jnp.asarray(table, BF16)


class Gather:
    def __init__(self, source, slots, sems, half):
        me = lax.axis_index("tensor")
        self.x, self.y = {"tensor": me ^ 1}, {"tensor": me ^ 2}
        self.source, self.slots, self.sems, self.half = source, slots, sems, half
        self.first = [
            self.copy(source, slots(0), 0, self.x),
            self.copy(source, slots(1), 1, self.y),
        ]
        self.second = [
            self.copy(half(slots(0), 0), half(slots(2), 0), 2, self.y),
            self.copy(half(slots(1), 1), half(slots(2), 1), 3, self.x),
        ]

    def copy(self, src, dst, i, to):
        return pltpu.make_async_remote_copy(
            src, dst, self.sems.at[0, i], self.sems.at[1, i], device_id=to, device_id_type=MESH
        )

    def start(self):
        for c in self.first:
            c.start()

    def forward(self):
        for c, d in zip(self.first, self.second):
            c.wait_recv()
            d.start()

    def finish(self):
        for d in self.second:
            d.wait_recv()
        for c in self.first + self.second:
            c.wait_send()


def greet(devices):
    barrier = pltpu.get_barrier_semaphore()
    for d in devices:
        pl.semaphore_signal(barrier, inc=1, device_id=d, device_id_type=MESH)
    pl.semaphore_wait(barrier, len(devices))


def features(rows, first, second, table, scaled):
    a = dot(rows, first) + table[0:1]
    b = dot(rows, second) + table[1:2]
    out = a * b
    return out * table[2:3] if scaled else out


def head_of(rows, h):
    lane = lax.broadcasted_iota(jnp.int32, rows.shape, 1)
    return jnp.where(lane // F == h, rows, jnp.zeros_like(rows))


def attention_forward(
    nz,
    x_ref,
    gain_ref,
    wqk_ref,
    wv_ref,
    wo_ref,
    spread_ref,
    e1_ref,
    e2_ref,
    table_ref,
    qk_ref,
    kq_ref,
    v_ref,
    yx_ref,
    y_ref,
    pre_ref,
    yall_ref,
    woall_ref,
    sloc,
    pout,
    gsems,
    wsems,
    csems,
    zsems,
):
    seqs, block, width = x_ref.shape
    heads = wqk_ref.shape[0] // (2 * F)
    value = wv_ref.shape[0] // heads
    z = lax.axis_index("seq")
    t = lax.axis_index("tensor")
    core = lax.axis_index("dp")
    side = lax.rem(core, 2)
    mate = {"dp": core + 1 - 2 * side}
    up, down = {"seq": lax.rem(z + 1, nz)}, {"seq": lax.rem(z + nz - 1, nz)}
    greet([{"tensor": t ^ 1}, {"tensor": t ^ 2}, mate, up, down])

    wrows = wo_ref.shape[0] // 2
    mine = pl.ds(pl.multiple_of(side * wrows, 16), wrows)
    wo = Gather(
        wo_ref.at[mine],
        lambda s: woall_ref.at[s, mine],
        wsems,
        lambda ref, i: ref.at[pl.ds(i * (wrows // 2), wrows // 2)],
    )
    wo.start()
    swaps = [
        pltpu.make_async_remote_copy(
            woall_ref.at[s, mine],
            woall_ref.at[s, mine],
            csems.at[0, s],
            csems.at[1, s],
            device_id=mate,
            device_id_type=MESH,
        )
        for s in range(3)
    ]
    table = table_ref[...]
    ones = jnp.where(
        lax.rem(lax.broadcasted_iota(jnp.int32, (1, heads * LANES), 1), LANES) == value, 1.0, 0.0
    )
    tile = block // 2

    def project(b, i):
        at = pl.ds(i * tile, tile)
        flat = pl.ds(b * block + i * tile, tile)
        rows = x_ref[b, at].astype(F32)
        normed = rows * lax.rsqrt(jnp.mean(rows * rows, axis=-1, keepdims=True) + 1e-06)
        normed = (normed * gain_ref[...]).astype(BF16)
        qk = dot(normed, wqk_ref[...], NT)
        qk_ref[flat] = qk.astype(BF16)
        kq_ref[flat] = pltpu.roll(qk, heads * F, 1).astype(BF16)
        values = dot(normed, wv_ref[...], NT).astype(BF16)
        v_ref[flat] = (dot(values, spread_ref[...]) + ones).astype(BF16)

    def lanes(h, n):
        return pl.ds(h * n, n)

    def states(b):
        flat = pl.ds(b * block, block)
        for h in range(heads):
            wide = lanes(h, WIDE)
            phi = features(kq_ref[flat], e1_ref[:, wide], e2_ref[:, wide], table, False)
            s = dot(phi.astype(BF16), v_ref[flat, lanes(h, LANES)], TN)
            sloc[b * heads + h] = s[:FEATS]

    def send_up(j):
        return pltpu.make_async_remote_copy(
            pout.at[j],
            pre_ref.at[j],
            zsems.at[0, j],
            zsems.at[1, j],
            device_id=up,
            device_id_type=MESH,
        )

    def chain(b, who):
        for at in who:

            @pl.when(z == at)
            def _():
                for h in range(heads):
                    j = b * heads + h
                    if at == 0:
                        pre_ref[j] = jnp.zeros((FEATS, LANES), BF16)
                        pout[j] = sloc[j].astype(BF16)
                    else:
                        send_up(j).wait_recv()
                        if at < nz - 1:
                            pout[j] = (sloc[j] + pre_ref[j].astype(F32)).astype(BF16)
                    if at < nz - 1:
                        send_up(j).start()

    def attend(b, h):
        narrow = lanes(h, LANES)
        wide = lanes(h, WIDE)
        for i in range(2):
            span = (i + 1) * tile
            at = pl.ds(b * block + i * tile, tile)
            until = pl.ds(b * block, span)
            rows = qk_ref[at]
            s = dot(head_of(rows, h), kq_ref[until], NT)
            w = 1.0 + s * (1.0 / math.sqrt(F))
            w = 0.5 * (w * w) + 0.5
            row = lax.broadcasted_iota(jnp.int32, w.shape, 0) + i * tile
            col = lax.broadcasted_iota(jnp.int32, w.shape, 1)
            w = jnp.where(col <= row, w, 0.0).astype(BF16)
            num = dot(w, v_ref[until, narrow])
            phi = features(rows, e1_ref[:, wide], e2_ref[:, wide], table, True)
            num = num + dot(phi[:, :FEATS].astype(BF16), pre_ref[b * heads + h])
            recip = 1.0 / num[:, value : value + 1]
            lane = lax.broadcasted_iota(jnp.int32, num.shape, 1)
            yx_ref[at, narrow] = jnp.where(lane == value, recip, num * recip)

    def gather(b):
        flat = pl.ds(b * block, block)
        return Gather(
            y_ref.at[flat],
            lambda s: yall_ref.at[s, flat],
            gsems.at[b],
            lambda ref, i: ref.at[pl.ds(i * tile, tile)],
        )

    def pack(b):
        for i in range(2):
            at = pl.ds(b * block + i * tile, tile)
            y_ref[at] = dot(yx_ref[at].astype(BF16), spread_ref[...], NT).astype(BF16)

    gathers = [gather(b) for b in range(seqs)]
    mid = list(range(1, nz - 1))
    for b in range(seqs + 1):
        if b < seqs:
            for i in range(2):
                project(b, i)
                if b > 0 and i == 0:
                    chain(b - 1, mid[:1])
            if b > 0:
                chain(b - 1, mid[1:])
            states(b)
            chain(b, [0])
        if b > 0:
            chain(b - 1, [nz - 1])
            for h in range(heads):
                attend(b - 1, h)
                if b == seqs - 1:
                    chain(b, mid[h : h + 1] if h < heads - 1 else mid[h:])
            pack(b - 1)
            gathers[b - 1].start()
    wo.forward()
    for s in range(2):
        swaps[s].start()
    for g in gathers:
        g.forward()
    wo.finish()
    swaps[2].start()
    for g in gathers:
        g.finish()
    for s in swaps:
        s.wait()

    @pl.when(z < nz - 1)
    def _():
        for j in range(seqs * heads):
            send_up(j).wait_send()


def run_attention_forward(x, gain, wqk, wv, wo, tables):
    seqs, block, width = x.shape
    heads = wqk.shape[0] // (2 * F)
    value = wv.shape[0] // heads
    rows = seqs * block
    spread, e1, e2, table = tables
    shapes = [
        jax.ShapeDtypeStruct((rows, 2 * heads * F), BF16),
        jax.ShapeDtypeStruct((rows, 2 * heads * F), BF16),
        jax.ShapeDtypeStruct((rows, heads * LANES), BF16),
        jax.ShapeDtypeStruct((rows, heads * LANES), F32),
        jax.ShapeDtypeStruct((rows, heads * value), BF16),
        jax.ShapeDtypeStruct((seqs * heads, FEATS, LANES), BF16),
        jax.ShapeDtypeStruct((3, rows, heads * value), BF16),
        jax.ShapeDtypeStruct((3,) + wo.shape, BF16),
    ]
    return pl.pallas_call(
        functools.partial(attention_forward, lax.axis_size("seq")),
        out_shape=shapes,
        in_specs=[VMEM_SPEC] * 9,
        out_specs=[VMEM_SPEC] * 6 + [ANY_SPEC] * 2,
        scratch_shapes=[
            pltpu.VMEM((seqs * heads, FEATS, LANES), F32),
            pltpu.VMEM((seqs * heads, FEATS, LANES), BF16),
            pltpu.SemaphoreType.DMA((seqs, 2, 4)),
            pltpu.SemaphoreType.DMA((2, 4)),
            pltpu.SemaphoreType.DMA((2, 3)),
            pltpu.SemaphoreType.DMA((2, seqs * heads)),
        ],
        compiler_params=pltpu.CompilerParams(
            collective_id=0, has_side_effects=True, vmem_limit_bytes=VMEM_LIMIT
        ),
        cost_estimate=pl.CostEstimate(
            flops=2 * rows * width * heads * (2 * F + value), bytes_accessed=20 << 20, transcendentals=0
        ),
        name="attention_forward",
    )(x, gain.reshape(1, width), wqk, wv, wo, spread, e1, e2, table)


class Exchange:
    def __init__(self, sems):
        me = lax.axis_index("tensor")
        self.x, self.y = {"tensor": me ^ 1}, {"tensor": me ^ 2}
        self.sems = sems

    def copy(self, src, dst, i, to):
        return pltpu.make_async_remote_copy(
            src, dst, self.sems.at[0, i], self.sems.at[1, i], device_id=to, device_id_type=MESH
        )


def rows_at(start, count):
    return pl.ds(pl.multiple_of(start, 16), count)


class ReduceScatter(Exchange):
    def __init__(self, part, near, far, sems):
        super().__init__(sems)
        me = lax.axis_index("tensor")
        self.part, self.near, self.far = part, near, far
        self.q = q = near.shape[1] * 2
        self.half = q // 2
        self.at = [me * q, (me ^ 1) * q, (me ^ 2) * q, (me ^ 3) * q]
        over = self.at[3]
        self.first = [
            self.copy(part.at[rows_at(over, self.half)], near.at[0], 0, self.x),
            self.copy(part.at[rows_at(over + self.half, self.half)], near.at[1], 1, self.y),
        ]
        self.second = [
            self.copy(part.at[rows_at(self.at[2], q)], far.at[1], 2, self.y),
            self.copy(part.at[rows_at(self.at[1], q)], far.at[0], 3, self.x),
        ]

    def start(self):
        for c in self.first:
            c.start()

    def forward(self):
        for i, start in ((0, self.at[2]), (1, self.at[1] + self.half)):
            self.first[i].wait_recv()
            rows = rows_at(start, self.half)
            self.part[rows] = (self.part[rows].astype(F32) + self.near[i].astype(F32)).astype(BF16)
            self.second[i].start()

    def finish(self):
        for c in self.second:
            c.wait_recv()

    def total(self, start, count):
        mine = self.part[rows_at(self.at[0] + start, count)].astype(F32)
        at = pl.ds(start, count)
        return mine + self.far[0, at].astype(F32) + self.far[1, at].astype(F32)

    def drain(self):
        for c in self.first + self.second:
            c.wait_send()


class RowGather(Exchange):
    def __init__(self, source, piece, half, sems):
        super().__init__(sems)
        me = lax.axis_index("tensor")
        self.first = [
            self.copy(source, piece(me), 0, self.x),
            self.copy(source, piece(me), 1, self.y),
        ]
        self.second = [
            self.copy(half(me ^ 1, 0), half(me ^ 1, 0), 2, self.y),
            self.copy(half(me ^ 2, 1), half(me ^ 2, 1), 3, self.x),
        ]

    start = Gather.start
    forward = Gather.forward
    finish = Gather.finish


def norm_backward(rows, grad, gain):
    norm = lax.rsqrt(jnp.mean(rows * rows, axis=-1, keepdims=True) + 1e-06)
    unit = rows * norm
    gain_grad = jnp.sum(grad * unit, axis=0, keepdims=True)
    scaled = grad * gain
    mean = jnp.mean(scaled * unit, axis=-1, keepdims=True)
    return norm * (scaled - unit * mean), gain_grad


def mlp_kernel(
    x_hbm,
    y_hbm,
    yall_hbm,
    wo_hbm,
    woall_hbm,
    wg_hbm,
    wu_hbm,
    wd_hbm,
    cot_hbm,
    gain_ref,
    len_ref,
    hidden_ref,
    r_ref,
    gr_ref,
    gain_grad_ref,
    gattn_hbm,
    gsum_hbm,
    land_hbm,
    wo4,
    wg,
    wu,
    wd,
    xt,
    yt,
    ct,
    h2t,
    gmt,
    gg,
    gu,
    part,
    near,
    far,
    ga,
    stage,
    back,
    lsems,
    rsems,
    asems,
    msems,
    bsems,
):
    seqs, block, width = x_hbm.shape
    tile = xt.shape[0]
    per = block // tile
    quarter = block // 4
    tiles = seqs * per
    ff = wg.shape[0]
    z = lax.axis_index("seq")
    t = lax.axis_index("tensor")
    core = lax.axis_index("dp")
    side = lax.rem(core, 2)
    mate = {"dp": core + 1 - 2 * side}
    greet([{"tensor": t ^ 1}, {"tensor": t ^ 2}, mate])
    gain = gain_ref[...]

    def load(src, dst, i):
        return pltpu.make_async_copy(src, dst, lsems.at[i])

    weights = [
        load(wo_hbm, wo4.at[0], 0),
        *[load(woall_hbm.at[s], wo4.at[s + 1], 1 + s) for s in range(3)],
        load(wg_hbm, wg, 4),
        load(wu_hbm, wu, 5),
        load(wd_hbm, wd, 6),
    ]

    def xy_loads(i):
        b, at = i // per, lax.rem(i, per) * tile
        flat = rows_at(i * tile, tile)
        return [
            load(x_hbm.at[b, rows_at(at, tile)], xt, 7),
            load(y_hbm.at[flat], yt.at[0], 8),
            *[load(yall_hbm.at[s, flat], yt.at[s + 1], 9 + s) for s in range(3)],
        ]

    def c_load(i):
        b, at = i // per, lax.rem(i, per) * tile
        return load(cot_hbm.at[b, rows_at(at, tile)], ct, 12)

    for c in xy_loads(0):
        c.start()
    for c in weights[:4]:
        c.start()
    for c in weights[4:6]:
        c.start()
    c_load(0).start()
    weights[6].start()
    quarters = [
        load(cot_hbm.at[b, rows_at(t * quarter, quarter)], ct.at[pl.ds(b * quarter, quarter)], 13 + b)
        for b in range(seqs)
    ]

    def mask(b, start, count):
        at = z * block + start + lax.broadcasted_iota(jnp.int32, (count, 1), 0)
        return (at < len_ref[b]).astype(F32)

    scatters = [
        ReduceScatter(part.at[pl.ds(b * block, block)], near.at[b], far.at[b], rsems.at[b])
        for b in range(seqs)
    ]
    gathers = []
    for b in range(seqs):

        def piece(i, b=b):
            return gattn_hbm.at[rows_at(b * block + i * quarter, quarter)]

        def half(i, h, b=b):
            return gattn_hbm.at[rows_at(b * block + i * quarter + h * (quarter // 2), quarter // 2)]

        gathers.append(RowGather(ga.at[b], piece, half, asems.at[b]))
    own_rows = [
        pltpu.make_async_copy(
            ga.at[b], gattn_hbm.at[rows_at(b * block + t * quarter, quarter)], bsems.at[b]
        )
        for b in range(seqs)
    ]

    def tile_step(i, first):
        b = i // per
        local = lax.rem(i, per)
        flat = rows_at(i * tile, tile)
        for c in xy_loads(i):
            c.wait()
        if first:
            for c in weights[:4]:
                c.wait()
        r = xt[...].astype(F32)
        for s in range(4):
            r = r + dot(yt[s], wo4[s])

        @pl.when(i + 1 < tiles)
        def _():
            for c in xy_loads(i + 1):
                c.start()

        @pl.when(t // 2 == local)
        def _():
            r_ref[b] = jnp.where(lax.rem(t, 2) == 0, r[:quarter], r[quarter:])

        h2 = r * lax.rsqrt(jnp.mean(r * r, axis=-1, keepdims=True) + 1e-06) * gain
        h2 = h2.astype(BF16)
        cols = pl.ds(pl.multiple_of(i * tile, LANES), tile)
        h2t[:, cols] = h2.T
        if first:
            for c in weights[4:6]:
                c.wait()
        gate = dot(h2, wg[...], NT)
        up = dot(h2, wu[...], NT)
        c_load(i).wait()
        gm = (ct[...].astype(F32) * mask(b, local * tile, tile)).astype(BF16)
        gmt[:, cols] = gm.T
        if first:
            weights[6].wait()
        gh = dot(gm, wd[...], NT)

        @pl.when(i + 1 < tiles)
        def _():
            c_load(i + 1).start()

        sig = 1.0 / (1.0 + jnp.exp(-gate))
        silu = gate * sig
        hidden_ref[flat] = (silu * up).astype(BF16)
        gg[flat] = (gh * up * (sig * (1.0 + gate * (1.0 - sig)))).astype(BF16)
        gu[flat] = (gh * silu).astype(BF16)
        part[flat] = (dot(gg[flat], wg[...]) + dot(gu[flat], wu[...])).astype(BF16)

    tile_step(0, True)

    def rest(i, carry):
        tile_step(i, False)
        for b in range(seqs):

            @pl.when(i == (b + 1) * per - 1)
            def _():
                scatters[b].start()

            if b < seqs - 1:

                @pl.when(i == (b + 1) * per)
                def _():
                    scatters[b].forward()

        return carry

    lax.fori_loop(1, tiles, rest, 0)
    for c in quarters:
        c.start()

    def mixed(b):
        scatters[b].finish()
        quarters[b].wait()
        grad = scatters[b].total(0, quarter)
        out = ct[pl.ds(b * quarter, quarter)].astype(F32) * mask(b, t * quarter, quarter)
        gr, gain_grad = norm_backward(r_ref[b], grad, gain)
        gr = gr + out
        gr_ref[b] = gr
        ga[b] = gr.astype(BF16)
        if b == 0:
            gain_grad_ref[...] = gain_grad
        else:
            gain_grad_ref[...] += gain_grad
        gathers[b].start()
        own_rows[b].start()

    mixed(0)
    lefts = (h2t, h2t, gmt)
    rights = (gg, gu, hidden_ref)
    half_rows = width // 2
    piece_rows = stage.shape[1]
    pieces = half_rows // piece_rows

    def product(base, n, m):
        return dot(lefts[n][rows_at(base + m * piece_rows, piece_rows)], rights[n][...])

    def to_mate(n, m):
        slot = (n * pieces + m) % 2
        return pltpu.make_async_remote_copy(
            stage.at[slot],
            land_hbm.at[n, rows_at(m * piece_rows, piece_rows)],
            msems.at[0, slot],
            msems.at[1, n * pieces + m],
            device_id=mate,
            device_id_type=MESH,
        )

    def from_mate(n, m):
        return pltpu.make_async_copy(
            land_hbm.at[n, rows_at(m * piece_rows, piece_rows)], back, bsems.at[2]
        )

    def to_sum(n, m):
        slot = (n * pieces + m) % 2
        return pltpu.make_async_copy(
            stage.at[slot], gsum_hbm.at[n, rows_at(m * piece_rows, piece_rows)], bsems.at[3 + slot]
        )

    work = [(n, m) for n in range(3) for m in range(pieces)]
    steps = [lambda: scatters[1].forward(), lambda: gathers[0].forward(), None, lambda: mixed(1)]
    for k, (n, m) in enumerate(work):
        out = product((1 - side) * half_rows, n, m)
        if k >= 2:
            to_mate(*work[k - 2]).wait_send()
        stage[k % 2] = out.astype(BF16)
        to_mate(n, m).start()
        if k < len(steps) and steps[k] is not None:
            steps[k]()
    for k in (len(work) - 2, len(work) - 1):
        to_mate(*work[k]).wait_send()
    for k, (n, m) in enumerate(work):
        to_mate(n, m).wait_recv()
        from_mate(n, m).start()
        out = product(side * half_rows, n, m)
        from_mate(n, m).wait()
        out = out + back[...].astype(F32)
        if k >= 2:
            to_sum(*work[k - 2]).wait()
        stage[k % 2] = out.astype(BF16)
        to_sum(n, m).start()
    for k in (len(work) - 2, len(work) - 1):
        to_sum(*work[k]).wait()
    gathers[1].forward()
    for b in range(seqs):
        own_rows[b].wait()
        gathers[b].finish()
        scatters[b].drain()


def run_mlp(x, y, yall, wo, woall, wg, wu, wd, cot, gain, lengths):
    seqs, block, width = x.shape
    rows = seqs * block
    value, ff = wo.shape[0], wg.shape[1]
    tile, quarter = block // 2, block // 4
    piece_rows = width // 8
    shapes = [
        jax.ShapeDtypeStruct((rows, ff), BF16),
        jax.ShapeDtypeStruct((seqs, quarter, width), F32),
        jax.ShapeDtypeStruct((seqs, quarter, width), F32),
        jax.ShapeDtypeStruct((1, width), F32),
        jax.ShapeDtypeStruct((rows, width), BF16),
        jax.ShapeDtypeStruct((3, width // 2, ff), BF16),
        jax.ShapeDtypeStruct((3, width // 2, ff), BF16),
    ]
    vm = pltpu.VMEM
    scratch = [
        vm((4, value, width), BF16),
        vm((ff, width), BF16),
        vm((ff, width), BF16),
        vm((ff, width), BF16),
        vm((tile, width), BF16),
        vm((4, tile, value), BF16),
        vm((tile, width), BF16),
        vm((width, rows), BF16),
        vm((width, rows), BF16),
        vm((rows, ff), BF16),
        vm((rows, ff), BF16),
        vm((rows, width), BF16),
        vm((seqs, 2, quarter // 2, width), BF16),
        vm((seqs, 2, quarter, width), BF16),
        vm((seqs, quarter, width), BF16),
        vm((2, piece_rows, ff), BF16),
        vm((piece_rows, ff), BF16),
        pltpu.SemaphoreType.DMA((15,)),
        pltpu.SemaphoreType.DMA((seqs, 2, 4)),
        pltpu.SemaphoreType.DMA((seqs, 2, 4)),
        pltpu.SemaphoreType.DMA((2, 12)),
        pltpu.SemaphoreType.DMA((5,)),
    ]
    return pl.pallas_call(
        mlp_kernel,
        out_shape=shapes,
        in_specs=[ANY_SPEC] * 9 + [VMEM_SPEC, pl.BlockSpec(memory_space=pltpu.SMEM)],
        out_specs=[VMEM_SPEC] * 4 + [ANY_SPEC] * 3,
        scratch_shapes=scratch,
        compiler_params=pltpu.CompilerParams(
            collective_id=1, has_side_effects=True, vmem_limit_bytes=VMEM_LIMIT
        ),
        cost_estimate=pl.CostEstimate(
            flops=2 * rows * width * (4 * value + 8 * ff), bytes_accessed=60 << 20, transcendentals=0
        ),
        name="mlp_forward_backward",
    )(x, y, yall, wo, woall, wg.T, wu.T, wd, cot, gain.reshape(1, width), lengths)


def attention_backward(
    nz,
    x_hbm,
    gain_ref,
    qk_ref,
    kq_ref,
    v_ref,
    yx_ref,
    pre_ref,
    gattn_ref,
    wo_ref,
    wqk_ref,
    wv_ref,
    gr_ref,
    gains_ref,
    spread_ref,
    e1_ref,
    e2_ref,
    f1_ref,
    f2_ref,
    table_ref,
    grads_ref,
    gains_out,
    gt_hbm,
    gn,
    gv,
    gvb,
    gqk,
    gqkb,
    yb,
    gat,
    h1t,
    sloc,
    sout,
    suf,
    xt,
    xq,
    part,
    near,
    far,
    gq,
    stage,
    land,
    total,
    zland,
    gsend,
    gland,
    lsems,
    zsems,
    rsems,
    asems,
    msems,
    dsems,
    ksems,
):
    seqs, block, width = x_hbm.shape
    heads = wqk_ref.shape[0] // (2 * F)
    value = wv_ref.shape[0] // heads
    tile, quarter = block // 2, block // 4
    rows = seqs * block
    z = lax.axis_index("seq")
    t = lax.axis_index("tensor")
    core = lax.axis_index("dp")
    side = lax.rem(core, 2)
    mate = {"dp": core + 1 - 2 * side}
    others = [{"seq": lax.rem(z + k, nz)} for k in range(1, nz)]
    greet([{"tensor": t ^ 1}, {"tensor": t ^ 2}, mate] + others)
    down = others[-1]
    gain = gain_ref[...]
    table = table_ref[...]
    scale = table[2:3, :FEATS]

    def lanes(h, n):
        return pl.ds(h * n, n)

    def x_load(i):
        b, at = i // 2, (i % 2) * tile
        return pltpu.make_async_copy(x_hbm.at[b, pl.ds(at, tile)], xt.at[i % 2], lsems.at[i % 2])

    quarters = [
        pltpu.make_async_copy(
            x_hbm.at[b, rows_at(t * quarter, quarter)], xq.at[b], lsems.at[2 + b]
        )
        for b in range(seqs)
    ]
    x_load(0).start()
    x_load(1).start()
    for c in quarters:
        c.start()

    def value_grads(i):
        at = pl.ds(i * tile, tile)
        ga = gattn_ref[at]
        gy = dot(dot(ga, wo_ref[...], NT).astype(BF16), spread_ref[...])
        gat[:, pl.ds(i * tile, tile)] = ga.T
        yb[at] = yx_ref[at].astype(BF16)
        for h in range(heads):
            narrow = lanes(h, LANES)
            g, y = gy[:, h * LANES : (h + 1) * LANES], yx_ref[at, narrow]
            recip = y[:, value : value + 1]
            den = -jnp.sum(g * y, axis=-1, keepdims=True)
            lane = lax.broadcasted_iota(jnp.int32, g.shape, 1)
            gn[at, narrow] = (jnp.where(lane == value, den, g) * recip).astype(BF16)

    def expand(ref, at, h):
        a = dot(ref[at], e1_ref[:, h * WIDE : h * WIDE + FEATS]) + table[0:1, :FEATS]
        b = dot(ref[at], e2_ref[:, h * WIDE : h * WIDE + FEATS]) + table[1:2, :FEATS]
        return a, b

    def states(b):
        flat = pl.ds(b * block, block)
        for h in range(heads):
            a, c = expand(qk_ref, flat, h)
            phi = (a * c * scale).astype(BF16)
            sloc[b * heads + h] = dot(phi, gn[flat, lanes(h, LANES)], TN)

    def send_down(j):
        return pltpu.make_async_remote_copy(
            sout.at[j], suf.at[j], zsems.at[0, j], zsems.at[1, j], device_id=down, device_id_type=MESH
        )

    def chain(b, who):
        for at in who:

            @pl.when(z == nz - 1 - at)
            def _():
                for h in range(heads):
                    j = b * heads + h
                    if at == 0:
                        suf[j] = jnp.zeros((FEATS, LANES), BF16)
                        sout[j] = sloc[j].astype(BF16)
                    else:
                        send_down(j).wait_recv()
                        if at < nz - 1:
                            sout[j] = (sloc[j] + suf[j].astype(F32)).astype(BF16)
                    if at < nz - 1:
                        send_down(j).start()

    def contract(a, c, grad, h, first, second):
        wide = slice(h * WIDE, h * WIDE + FEATS)
        return dot((grad * c).astype(BF16), first[:, wide], NT) + dot(
            (grad * a).astype(BF16), second[:, wide], NT
        )

    def local(b, h):
        narrow = lanes(h, LANES)
        for i in range(2):
            span = (i + 1) * tile
            at = pl.ds(b * block + i * tile, tile)
            until = pl.ds(b * block, span)
            s = dot(head_of(qk_ref[at], h), kq_ref[until], NT)
            w = 1.0 + s * (1.0 / math.sqrt(F))
            row = lax.broadcasted_iota(jnp.int32, w.shape, 0) + i * tile
            col = lax.broadcasted_iota(jnp.int32, w.shape, 1)
            seen = col <= row
            kernel = jnp.where(seen, 0.5 * (w * w) + 0.5, 0.0).astype(BF16)
            grad = gn[at, narrow]
            gs = dot(grad, v_ref[until, narrow], NT) * (w * (1.0 / math.sqrt(F)))
            gs = jnp.where(seen, gs, 0.0).astype(BF16)
            gv[until, narrow] += dot(kernel, grad, TN)
            gqk[until] += dot(gs, head_of(kq_ref[at], heads + h), TN)
            a, c = expand(qk_ref, at, h)
            gphi = dot(grad, pre_ref[b * heads + h], NT) * scale
            gqk[at] += dot(gs, head_of(kq_ref[until], h)) + contract(a, c, gphi, h, e1_ref, e2_ref)

    def state_grads(b, h):
        narrow = lanes(h, LANES)
        flat = pl.ds(b * block, block)
        later = suf[b * heads + h]
        a, c = expand(kq_ref, flat, h)
        gphi = dot(v_ref[flat, narrow], later, NT)
        gqk[flat] += contract(a, c, gphi, h, f1_ref, f2_ref)
        gv[flat, narrow] += dot((a * c).astype(BF16), later)

    def norm_grads(b):
        for i in range(2):
            at = pl.ds(b * block + i * tile, tile)
            gvb[at] = gv[at].astype(BF16)
            gqkb[at] = gqk[at].astype(BF16)
            packed = dot(gvb[at], spread_ref[...], NT).astype(BF16)
            part[at] = (dot(gqkb[at], wqk_ref[...]) + dot(packed, wv_ref[...])).astype(BF16)

    def normed_rows(i):
        x_load(i).wait()
        r = xt[i % 2].astype(F32)
        h1 = r * lax.rsqrt(jnp.mean(r * r, axis=-1, keepdims=True) + 1e-06) * gain
        h1t[:, pl.ds(i * tile, tile)] = h1.astype(BF16).T
        if i + 2 < 2 * seqs:
            x_load(i + 2).start()

    scatters = [
        ReduceScatter(part.at[pl.ds(b * block, block)], near.at[b], far.at[b], rsems.at[b])
        for b in range(seqs)
    ]
    gathers = []
    for b in range(seqs):

        def piece(i, b=b):
            return gt_hbm.at[b, rows_at(i * quarter, quarter)]

        def half(i, h, b=b):
            return gt_hbm.at[b, rows_at(i * quarter + h * (quarter // 2), quarter // 2)]

        gathers.append(RowGather(gq.at[b], piece, half, asems.at[b]))
    own_rows = [
        pltpu.make_async_copy(gq.at[b], gt_hbm.at[b, rows_at(t * quarter, quarter)], lsems.at[4 + b])
        for b in range(seqs)
    ]

    half_rows = width // 2
    chunk = half_rows // nz
    spans = [pl.ds(0, heads * LANES), pl.ds(heads * LANES, 2 * heads * F + heads * LANES)]

    def product(p, base):
        at = rows_at(base, half_rows)
        if p == 0:
            return dot(gat[at], yb[...])
        return jnp.concatenate([dot(h1t[at], gqkb[...]), dot(h1t[at], gvb[...])], axis=1)

    def to_mate(p):
        return pltpu.make_async_remote_copy(
            stage.at[:, spans[p]],
            land.at[:, spans[p]],
            msems.at[0, p],
            msems.at[1, p],
            device_id=mate,
            device_id_type=MESH,
        )

    def to_chunks(p):
        return [
            pltpu.make_async_remote_copy(
                total.at[rows_at(lax.rem(z + k, nz) * chunk, chunk), spans[p]],
                zland.at[k - 1, :, spans[p]],
                dsems.at[0, p, k - 1],
                dsems.at[1, p, k - 1],
                device_id=others[k - 1],
                device_id_type=MESH,
            )
            for k in range(1, nz)
        ]

    def send_half(p):
        stage[:, spans[p]] = product(p, (1 - side) * half_rows).astype(BF16)
        to_mate(p).start()

    def sum_half(p):
        out = product(p, side * half_rows)
        to_mate(p).wait_recv()
        total[:, spans[p]] = (out + land[:, spans[p]].astype(F32)).astype(BF16)
        for c in to_chunks(p):
            c.start()

    def tokens(b):
        scatters[b].finish()
        quarters[b].wait()
        grad, gain_grad = norm_backward(
            xq[b].astype(F32), scatters[b].total(0, quarter), gain
        )
        gq[b] = (grad + gr_ref[b]).astype(BF16)
        gathers[b].start()
        own_rows[b].start()
        if b == 0:
            gsend[0] = jnp.concatenate(
                [gain_grad, gains_ref[...], jnp.zeros((6, width), F32)], axis=0
            )
        else:
            gsend[0, 0:1] += gain_grad

    gv[...] = jnp.zeros_like(gv)
    gqk[...] = jnp.zeros_like(gqk)
    mid = list(range(1, nz - 1))
    value_grads(0)
    value_grads(1)
    states(0)
    chain(0, [0])
    for b in range(1, seqs):
        value_grads(2 * b)
        chain(b - 1, mid[:1])
        value_grads(2 * b + 1)
        states(b)
        chain(b - 1, mid[1:])
        chain(b, [0])
    for b in range(seqs):
        for h in range(heads):
            local(b, h)
            if b == 0:
                chain(1, mid[h : h + 1] if h < heads - 1 else mid[h:])
        chain(b, [nz - 1])
        if b > 0:
            scatters[b - 1].forward()
        for h in range(heads):
            state_grads(b, h)
        norm_grads(b)
        scatters[b].start()
    send_half(0)
    tokens(0)
    for i in range(2 * seqs):
        normed_rows(i)
    scatters[1].forward()
    send_half(1)
    gathers[0].forward()
    sum_half(0)
    tokens(1)
    sum_half(1)

    hops = [{"tensor": t ^ 1}, {"tensor": t ^ 2}, mate]
    for i, to in enumerate(hops):
        c = pltpu.make_async_remote_copy(
            gsend.at[i], gland.at[i], ksems.at[0, i], ksems.at[1, i], device_id=to, device_id_type=MESH
        )
        c.start()
        c.wait()
        gsend[i + 1] = gsend[i] + gland[i]
    last = len(hops)
    copies = [
        pltpu.make_async_remote_copy(
            gsend.at[last],
            gland.at[last + k],
            ksems.at[0, last + k],
            ksems.at[1, last + k],
            device_id=others[k],
            device_id_type=MESH,
        )
        for k in range(nz - 1)
    ]
    for c in copies:
        c.start()
    gathers[1].forward()
    for p in range(2):
        for c in to_chunks(p):
            c.wait()
        out = total[rows_at(z * chunk, chunk), spans[p]].astype(F32)
        for k in range(nz - 1):
            out = out + zland[k, :, spans[p]].astype(F32)
        grads_ref[:, spans[p]] = out
        to_mate(p).wait_send()
    gains = gsend[last]
    for k, c in enumerate(copies):
        c.wait()
        gains = gains + gland[last + k]
    gains_out[...] = gains
    for b in range(seqs):
        own_rows[b].wait()
        gathers[b].finish()
        scatters[b].drain()

    @pl.when(z > 0)
    def _():
        for j in range(seqs * heads):
            send_down(j).wait_send()


def run_attention_backward(
    x, gain, qk, kq, v_ext, yx, pre, gattn, wo, wqk, wv, gr, gains, tables
):
    seqs, block, width = x.shape
    rows = seqs * block
    heads = wqk.shape[0] // (2 * F)
    quarter, tile = block // 4, block // 2
    nz = lax.axis_size("seq")
    spread, e1, e2, table = tables
    half = heads * F
    f1, f2 = jnp.roll(e1, half, 0), jnp.roll(e2, half, 0)
    chunk = width // 2 // nz
    cols = 2 * heads * LANES + 2 * heads * F
    shapes = [
        jax.ShapeDtypeStruct((chunk, cols), F32),
        jax.ShapeDtypeStruct((8, width), F32),
        jax.ShapeDtypeStruct(x.shape, BF16),
    ]
    vm, dma = pltpu.VMEM, pltpu.SemaphoreType.DMA
    wide = heads * LANES
    scratch = [
        vm((rows, wide), BF16),
        vm((rows, wide), F32),
        vm((rows, wide), BF16),
        vm((rows, 2 * half), F32),
        vm((rows, 2 * half), BF16),
        vm((rows, wide), BF16),
        vm((width, rows), BF16),
        vm((width, rows), BF16),
        vm((seqs * heads, FEATS, LANES), F32),
        vm((seqs * heads, FEATS, LANES), BF16),
        vm((seqs * heads, FEATS, LANES), BF16),
        vm((2, tile, width), BF16),
        vm((seqs, quarter, width), BF16),
        vm((rows, width), BF16),
        vm((seqs, 2, quarter // 2, width), BF16),
        vm((seqs, 2, quarter, width), BF16),
        vm((seqs, quarter, width), BF16),
        vm((width // 2, cols), BF16),
        vm((width // 2, cols), BF16),
        vm((width // 2, cols), BF16),
        vm((nz - 1, chunk, cols), BF16),
        vm((4, 8, width), F32),
        vm((3 + nz - 1, 8, width), F32),
        dma((4 + seqs,)),
        dma((2, seqs * heads)),
        dma((seqs, 2, 4)),
        dma((seqs, 2, 4)),
        dma((2, 2)),
        dma((2, 2, nz - 1)),
        dma((2, 3 + nz - 1)),
    ]
    return pl.pallas_call(
        functools.partial(attention_backward, nz),
        out_shape=shapes,
        in_specs=[ANY_SPEC] + [VMEM_SPEC] * 18,
        out_specs=[VMEM_SPEC] * 2 + [ANY_SPEC],
        scratch_shapes=scratch,
        compiler_params=pltpu.CompilerParams(
            collective_id=2, has_side_effects=True, vmem_limit_bytes=VMEM_LIMIT
        ),
        cost_estimate=pl.CostEstimate(
            flops=8 * rows * width * wide, bytes_accessed=30 << 20, transcendentals=0
        ),
        name="attention_backward",
    )(x, gain.reshape(1, width), qk, kq, v_ext, yx, pre, gattn, wo, wqk, wv, gr, gains, spread, e1, e2, f1, f2, table)


def shards(
    tokens,
    lengths,
    attn_gain,
    w_query,
    w_key,
    w_value,
    w_output,
    mlp_gain,
    w_gate,
    w_up,
    w_down,
    cotangent,
):
    seqs, block, width = tokens.shape
    heads = w_query.shape[1] // F
    value = w_value.shape[1] // heads
    quarter = block // 4
    chips = lax.axis_size("dp") // 2
    t = lax.axis_index("tensor")
    tables = (spread_table(heads, value),) + feature_tables(heads)
    wqk = jnp.concatenate([w_query.T, w_key.T], axis=0)
    wv = w_value.T
    qk, kq, v_ext, yx, y, pre, yall, woall = run_attention_forward(
        tokens, attn_gain, wqk, wv, w_output, tables
    )
    hidden, r_own, gr_own, mlp_gain_grad, grad_attn, gsum, _ = run_mlp(
        tokens, y, yall, w_output, woall, w_gate, w_up, w_down, cotangent, mlp_gain, lengths
    )
    attn_grads, gains, grad_tokens = run_attention_backward(
        tokens, attn_gain, qk, kq, v_ext, yx, pre, grad_attn, w_output, wqk, wv, gr_own, mlp_gain_grad, tables
    )

    mlp_part = dot(hidden, w_down).astype(BF16).reshape(seqs, block, width)
    mlp_out = lax.psum_scatter(mlp_part, "tensor", scatter_dimension=1, tiled=True).astype(F32)
    positions = lax.axis_index("seq") * block + t * quarter + jnp.arange(quarter, dtype=jnp.int32)
    mask = (positions[None, :] < lengths[:, None]).astype(F32)[:, :, None]
    block_out = lax.all_gather((mask * (r_own + mlp_out)).astype(BF16), "tensor", axis=1, tiled=True)

    if chips == 1:
        mlp_grads = [
            lax.psum_scatter(gsum[i], "seq", scatter_dimension=0, tiled=True).astype(F32)
            for i in range(3)
        ]
    else:
        pairs = [[2 * i, 2 * i + 1] for i in range(chips)]

        def scatter(a, copies):
            a = (a.astype(F32) * (1.0 / copies)).astype(BF16)
            return lax.psum_scatter(a, ("dp", "seq"), scatter_dimension=0, tiled=True).astype(F32)

        def joined(a, axis):
            return lax.all_gather(a, "dp", axis=axis, tiled=True, axis_index_groups=pairs)

        both = joined(gsum, 1)
        mlp_grads = [scatter(both[i], 2) for i in range(3)]
        whole = lax.all_gather(attn_grads.astype(BF16), "seq", axis=0, tiled=True)
        attn_grads = scatter(joined(whole, 0), 2 * lax.axis_size("seq"))
        gains = lax.psum(gains, "dp") * 0.5
    share = width // (lax.axis_size("dp") * lax.axis_size("seq"))
    place = (lax.axis_index("dp") * lax.axis_size("seq") + lax.axis_index("seq")) * share
    gains = lax.dynamic_slice_in_dim(gains, place, share, 1)

    def unspread(a):
        return a.reshape(share, heads, LANES)[:, :, :value].reshape(share, heads * value)

    edge, half = heads * LANES, heads * F
    return (
        block_out,
        grad_tokens.astype(F32),
        gains[0],
        attn_grads[:, edge : edge + half],
        attn_grads[:, edge + half : edge + 2 * half],
        unspread(attn_grads[:, edge + 2 * half :]),
        unspread(attn_grads[:, :edge]).T,
        gains[1],
        mlp_grads[0],
        mlp_grads[1],
        mlp_grads[2].T,
    )


def solution(mesh):
    in_specs = (
        P("dp", "seq", None),
        P("dp"),
        P(),
        P(None, "tensor"),
        P(None, "tensor"),
        P(None, "tensor"),
        P("tensor", None),
        P(),
        P(None, "tensor"),
        P(None, "tensor"),
        P("tensor", None),
        P("dp", "seq", None),
    )
    out_specs = (
        P("dp", "seq", None),
        P("dp", "seq", None),
        P(("dp", "seq")),
        P(("dp", "seq"), "tensor"),
        P(("dp", "seq"), "tensor"),
        P(("dp", "seq"), "tensor"),
        P("tensor", ("dp", "seq")),
        P(("dp", "seq")),
        P(("dp", "seq"), "tensor"),
        P(("dp", "seq"), "tensor"),
        P("tensor", ("dp", "seq")),
    )
    return jax.shard_map(shards, mesh=mesh, in_specs=in_specs, out_specs=out_specs, check_vma=False)
```

time: 1170 us -> 522 us (0.45)
  waiting for transfers between devices: 668 us -> 116 us
  Pallas kernels: 0 us -> 339 us
  matrix products: 198 us -> 9.77 us
  other arithmetic: 149 us -> 16.8 us
  local copies, waits for them, and re-layouts: 77.5 us -> 18.2 us
  blocking collectives: 45.5 us -> 0 us
    psum x3 -> x0, waiting for transfers between devices: 341 us -> none  [the longest x1 158 us: shards(): lax.psum(product(hidden, w_down, 'rf,fe->re').astype(jnp.bfloat16), 'tens...]
    pallas_call x0 -> x3, Pallas kernels: none -> 339 us  [the longest x1 146 us: run_attention_backward(): pl.pallas_call(functools.partial(attention_backward, nz), out_shape=shape...]
    reduce_scatter x4, waiting for transfers between devices: 324 us -> 66.6 us  [the longest x1 40.4 us: shards(): lax.psum_scatter(mlp_part, 'tensor', scatter_dimension=1, tiled=True)]
    dot_general x35 -> x1, matrix products: 198 us -> 9.77 us  [dot(): return lax.dot_general(a, b, dims, preferred_element_type=F32)]
    scatter-add x4 -> x0, other arithmetic: 62.5 us -> none  [feature_map(): pair_terms = values[..., upper_i] * values[..., upper_j] * pair_scale]
    all_gather x2 -> x1, waiting for transfers between devices: 2.2 us -> 48.3 us  [shards(): lax.all_gather((mask * (r_own + mlp_out)).astype(BF16), 'tensor', axis=1,...]
    all_gather x2 -> x0, blocking collectives: 28.2 us -> none  [carried_in(): lax.all_gather(part.astype(kind), axis)]
    reduce_sum x6 -> x0, other arithmetic: 22.6 us -> none  [the longest x2 12.4 us: rms_apply(): row_data * lax.rsqrt(jnp.mean(row_data * row_data, axis=-1, keepdims=True...]
  transfers between devices with their start and end apart: 12 -> 5, of which waited for: 8 -> 3; matrix products, arithmetic and copies ran while one was open for 16% -> 5% of each run, Pallas kernels for 0% -> 28%
where the time goes in v1:
time: 522 us; the launch traced here: 515 us
  Pallas kernels  339 us (65%)
  waiting for transfers between devices  116 us (22%)
  local copies, waits for them, and re-layouts  18.2 us (3%)
  other arithmetic  16.8 us (3%)
  between operations  14.3 us (3%)
  matrix products  9.77 us (2%)
    pallas_call x1, Pallas kernels, run_attention_backward(): pl.pallas_call(functools.partial(attention_backward, nz), out_shape=shape...  146 us
    pallas_call x1, Pallas kernels, run_mlp(): pl.pallas_call(mlp_kernel, out_shape=shapes, in_specs=[ANY_SPEC] * 9 + [V...  121 us
    pallas_call x1, Pallas kernels, run_attention_forward(): pl.pallas_call(functools.partial(attention_forward, lax.axis_size('seq'))...  72.7 us
    all_gather x1, waiting for transfers between devices, shards(): lax.all_gather((mask * (r_own + mlp_out)).astype(BF16), 'tensor', axis=1,...  48.3 us
    reduce_scatter x1, waiting for transfers between devices, shards(): lax.psum_scatter(mlp_part, 'tensor', scatter_dimension=1, tiled=True)  40.4 us
    reduce_scatter x3, waiting for transfers between devices, shards(): lax.psum_scatter(gsum[i], 'seq', scatter_dimension=0, tiled=True)  26.2 us
  transfers between devices with their start and end apart: 5, of which 3 were waited for; matrix products, arithmetic and copies ran while one was open for 5% of the time, Pallas kernels for 28%

profile of v1, /device:TPU:0, one launch (start us, length us, event | category | flops | bytes accessed | tf_op | source)
XLA Modules:
  0.0 514.7 jit_solution(18078399774698317339)
XLA Ops:
  7.2 1.3 reshape.77.gain_ref
  8.5 1.3 reshape.78.gain_ref
  9.8 1.8 pad_maximum_fusion.wqk_ref
  11.7 72.7 %attention_forward.1 = (bf16[1024,128]{1,0:T(8,128)(2,1)}, bf16[1024,128]{1,0:T(8,128)(2,1)}, bf16[1024,512]{1,0:T(8,128)(2,1)}, f32[1024,512]{1,0:T(8,128)}, bf...) custom-call(bf16[2,512,1792]{2,1,0:T(8,128)(2,1)} %x_hbm.3, ...), custom_call_target="tpu_custom_call" | custom-call | flops 2113929216 | bytes 20971520 | tf_op jit(solution)/shard_map/attention_forward/pallas_call | solution.py:313
  84.3 120.5 %mlp_forward_backward.1 = (bf16[1024,1216]{1,0:T(8,128)(2,1)}, f32[2,128,1792]{2,1,0:T(8,128)}, f32[2,128,1792]{2,1,0:T(8,128)}, f32[1,1792]{1,0:T(1,128)}, bf16...) custom-call(bf16[2,512,1792]{2,1,0:T(8,128)(2,1)} %x_hbm.3, ...), custom_call_target="tpu_custom_call" | custom-call | flops 42278584320 | bytes 62914560 | tf_op jit(solution)/shard_map/mlp_forward_backward/pallas_call | solution.py:730
  204.9 9.8 %convolution_convert_fusion = bf16[1024,1792]{1,0:T(8,128)(2,1)} fusion(bf16[1024,1216]{1,0:T(8,128)(2,1)} %get-tuple-element.32, bf16[1216,1792]{1,0:T(8,128)(2,1)} %wd_hbm.1), kind=kOutput, calls=%fused_computation | convolution fusion | flops 4464574464 | bytes 10518528 | tf_op jit(solution)/shard_map/dot_general | solution.py:28
  214.9 6.1 %slice_bitcast_fusion = (bf16[896,1216]{1,0:T(8,128)(2,1)}, bf16[896,1216]{1,0:T(8,128)(2,1)}, bf16[896,1216]{1,0:T(8,128)(2,1)}) fusion(bf16[3,896,1216]{2,1,0:T(8,128)(2,1)} %get-tuple-element.44), kind=kLoop, calls=%fused_computation.1 | loop fusion | bytes 13074432 | tf_op jit(solution)/shard_map/squeeze | solution.py:1208
  221.1 0.7 reduce-scatter.9.cloned.1.call-update
  221.8 0.5 reduce-scatter.11.cloned.1.call-update
  222.5 40.4 %reduce-scatter.5.cloned.1.call-done = bf16[2,128,1792]{2,1,0:T(8,128)(2,1)} async-done(((bf16[2,512,1792]{2,1,0:T(8,128)(2,1)}), bf16[2,128,1792]{2,1,0:T(8,128)(2,1)}) %reduce-scatter.5.cloned.1.call-update) | async-done | bytes 917520 | tf_op jit(solution)/shard_map/reduce_scatter | solution.py:1201
  262.9 2.4 multiply_convert_fusion
  265.2 146.0 %attention_backward.1 = (f32[224,1152]{1,0:T(8,128)}, f32[8,1792]{1,0:T(8,128)}, bf16[2,512,1792]{2,1,0:T(8,128)(2,1)}) custom-call(bf16[2,512,1792]{2,1,0:T(8,128)(2,1)} %x_hbm.3, f32[1,1792]{1,0:T(1,128)} %reshape.77.gain_ref, bf16[1024,128]{1,0:T(8,128)(2,1)} %get-tuple-element.33.qk_ref, bf16[1024,128]{1,0:T(8,128)(2,1)} %get-tuple-element.34.kq_ref, ...), custom_call_target="tpu_custom_call" | custom-call | flops 7516192768 | bytes 31457280 | tf_op jit(solution)/shard_map/attention_backward/pallas_call | solution.py:1151
  411.2 6.1 %convert_element_type.30 = f32[2,512,1792]{2,1,0:T(8,128)} convert(bf16[2,512,1792]{2,1,0:T(8,128)(2,1)} %get-tuple-element.41) | non-fusion elementwise | flops 1835008 | bytes 11010048 | tf_op jit(solution)/shard_map/convert_element_type | solution.py:1236
  417.6 1.0 copy.27
  418.8 1.0 reshape.81
  419.9 0.7 copy.28
  420.6 0.7 copy.29
  421.3 1.4 fusion.2
  422.7 2.1 convert_element_type.31
  424.9 2.1 convert_element_type.32
  427.0 26.2 %reduce-scatter.11.cloned.1.call-done = bf16[224,1216]{1,0:T(8,128)(2,1)} async-done(((bf16[896,1216]{1,0:T(8,128)(2,1)}), bf16[224,1216]{1,0:T(8,128)(2,1)}) %reduce-scatter.11.cloned.1.call-update) | async-done | bytes 544784 | tf_op jit(solution)/shard_map/reduce_scatter | solution.py:1208
  453.2 2.1 convert_bitcast_fusion
  455.4 48.3 %all-gather.2.cloned.1.call-done = bf16[2,512,1792]{2,1,0:T(8,128)(2,1)} async-done(((bf16[2,128,1792]{2,1,0:T(8,128)(2,1)}), bf16[2,512,1792]{2,1,0:T(8,128)(2,1)}) %all-gather.2.cloned.1.call-update) | async-done | bytes 3670032 | tf_op jit(solution)/shard_map/all_gather | solution.py:1204
  503.7 4.1 copy.31
  (22 shorter events, 1.0 us)
Async XLA Ops:
  7.2 255.7 %reduce-scatter.5.cloned.1.call-start = ((), (), s32[]{:S(2)}) async-start(), calls=%async_computation.4 | async-start | bytes 4587520 | tf_op jit(solution)/shard_map/reduce_scatter | solution.py:1201
  214.7 208.0 %reduce-scatter.7.cloned.1.call-start = ((), (), s32[]{:S(2)}) async-start(), calls=%async_computation.6 | async-start | bytes 2867200 | tf_op jit(solution)/shard_map/reduce_scatter | solution.py:1208
  221.0 1.4 copy-start.2
  221.0 41.8 %copy-start = (f32[2,128,1792]{2,1,0:T(8,128)S(1)}, f32[2,128,1792]{2,1,0:T(8,128)}, u32[]{:S(2)}) copy-start(f32[2,128,1792]{2,1,0:T(8,128)} %get-tuple-element.31) | copy-start | bytes 5505028
  221.0 203.8 %reduce-scatter.9.cloned.1.call-start = ((), (), s32[]{:S(2)}) async-start(), calls=%async_computation.7 | async-start | bytes 2867200 | tf_op jit(solution)/shard_map/reduce_scatter | solution.py:1208
  221.8 231.5 %reduce-scatter.11.cloned.1.call-start = ((), (), s32[]{:S(2)}) async-start(), calls=%async_computation.8 | async-start | bytes 2867200 | tf_op jit(solution)/shard_map/reduce_scatter | solution.py:1208
  222.4 281.3 %all-gather.2.cloned.1.call-start = ((), (), s32[]{:S(2)}) async-start(), calls=%async_computation.5 | async-start | bytes 4587520 | tf_op jit(solution)/shard_map/all_gather | solution.py:1204
  411.2 6.1 %copy-start.1 = (f32[224,1152]{1,0:T(8,128)S(1)}, f32[224,1152]{1,0:T(8,128)}, u32[]{:S(2)}) copy-start(f32[224,1152]{1,0:T(8,128)} %get-tuple-element.43) | copy-start | bytes 3096580
Sparse Core Ops, SparseCore 0:
  214.8 48.0 reduce-scatter.4
  265.2 53.8 reduce-scatter.6
  321.6 75.6 reduce-scatter.8
  399.5 53.7 reduce-scatter.10
  455.6 47.9 all-gather.1
